TPU v7x, 32 devices: a whole 2x2x4 slice. The times are simulated.
32 devices in a mesh: dom: 2 (over x), space: 16 (over z, y, core).
Axes of the slice: x: 2, y: 2, z: 4, core: 2. Of those that a mesh axis runs over, the one named last changes fastest.
Arguments:
- inputs: bfloat16 [2, 32, 2048, 2048], P('dom', None, 'space'), parts along dimension 0, may hold values from -10.5 to 10.5
- target: bfloat16 [2, 32, 2048, 2048], P('dom', None, 'space'), parts along dimension 0, may hold values from -6 to 6
- spectral_weight: float32 [64, 32, 32, 128], P('space'), may hold values from -18 to 18
- local_weight: bfloat16 [32, 32], replicated, may hold values from -1 to 1
- bias_term: float32 [32], replicated, may hold values from -3 to 3
Outputs:
- grad_input: bfloat16 [2, 32, 2048, 2048], P('dom', None, 'space'), parts along dimension 0
- grad_spectral: float32 [64, 64, 32, 128], P('space', 'dom'), parts along dimension 1
- grad_local: float32 [64, 32], P('dom'), parts along dimension 0
- grad_bias: float32 [64], P('dom'), parts along dimension 0
There are 2 independent parts, one for each index of `dom`. A program takes and returns all parts, laid end to end along the dimension named above; an argument that names none is the same for every part. Nothing has to cross between parts.
All inputs are finite; a program needn't handle non-finite values.
Results may differ from a plain program's by a relative error of at most 0.014.
Values may be sent and summed in bfloat16 or wider, within the bound.
A program may use at most 192 MiB of HBM per device.

v0:
```python
import math

import jax
import jax.numpy as jnp
from jax import lax
from jax.sharding import PartitionSpec as P

H = 2048
W = 2048
KX = 64
KY = 64


PRECISE = lax.Precision.HIGHEST


def row_table():
    mode_index = jnp.arange(KY, dtype=jnp.int32)[:, None]
    column = jnp.arange(W, dtype=jnp.int32)[None, :]
    angles = (mode_index * column % W).astype(jnp.float32) * (2.0 * math.pi / W)
    factor = 1.0 / math.sqrt(H * W)
    return jnp.stack([jnp.cos(angles) * factor, -jnp.sin(angles) * factor]).astype(jnp.bfloat16)


def column_table(row_index):
    column = jnp.arange(KX, dtype=jnp.int32)
    frequency = jnp.where(column < KX // 2, column, column + H - KX)
    angles = (row_index[:, None] * frequency[None, :] % H).astype(jnp.float32) * (2.0 * math.pi / H)
    return jnp.concatenate([jnp.cos(angles), jnp.sin(angles)], axis=1)


def mode_weights(start_mode, mode_count):
    mode_index = start_mode + jnp.arange(mode_count, dtype=jnp.int32)
    return jnp.where(mode_index == 0, 1.0, 2.0).astype(jnp.float32)


def row_analysis(field_data, basis):
    return jnp.einsum("schw,pkw->kpsch", field_data, basis, preferred_element_type=jnp.float32)


def row_synth(spectra, basis):
    return jnp.einsum("kpsch,pkw->schw", spectra, basis, preferred_element_type=jnp.float32)


def column_modes(slab_part, basis):
    product = jnp.einsum("kpsch,hj->kpscj", slab_part, basis, precision=PRECISE)
    half_count = basis.shape[1] // 2
    real_part = product[:, 0, :, :, :half_count] + product[:, 1, :, :, half_count:]
    imag_part = product[:, 1, :, :, :half_count] - product[:, 0, :, :, half_count:]
    return jnp.concatenate([real_part, imag_part], axis=-1)


def column_synth(mode_data, basis):
    half_count = basis.shape[1] // 2
    real_part, imag_part = (mode_data[..., :half_count], mode_data[..., half_count:])
    cosines, sine_part = (basis[:, :half_count], basis[:, half_count:])
    first_part = jnp.einsum("ysok,hk->ysoh", real_part, cosines, precision=PRECISE) - jnp.einsum(
        "ysok,hk->ysoh", imag_part, sine_part, precision=PRECISE
    )
    second = jnp.einsum("ysok,hk->ysoh", real_part, sine_part, precision=PRECISE) + jnp.einsum(
        "ysok,hk->ysoh", imag_part, cosines, precision=PRECISE
    )
    return jnp.stack([first_part, second], axis=1).astype(jnp.bfloat16)


def split_complex(mode_data):
    half_count = mode_data.shape[-1] // 2
    return (mode_data[..., :half_count], mode_data[..., half_count:])


def mix_modes(input_modes, weight):
    spec_real, spec_imag = split_complex(input_modes)
    weight_real, weight_imag = split_complex(weight)
    form = "ysck,ycok->ysok"
    out_real = jnp.einsum(form, spec_real, weight_real, precision=PRECISE) - jnp.einsum(
        form, spec_imag, weight_imag, precision=PRECISE
    )
    out_imag = jnp.einsum(form, spec_real, weight_imag, precision=PRECISE) + jnp.einsum(
        form, spec_imag, weight_real, precision=PRECISE
    )
    return jnp.concatenate([out_real, out_imag], axis=-1)


def mix_back(delta_modes, weight):
    delta_real, delta_imag = split_complex(delta_modes)
    weight_real, weight_imag = split_complex(weight)
    form = "ysok,ycok->ysck"
    out_real = jnp.einsum(form, delta_real, weight_real, precision=PRECISE) + jnp.einsum(
        form, delta_imag, weight_imag, precision=PRECISE
    )
    out_imag = jnp.einsum(form, delta_imag, weight_real, precision=PRECISE) - jnp.einsum(
        form, delta_real, weight_imag, precision=PRECISE
    )
    return jnp.concatenate([out_real, out_imag], axis=-1)


def mix_grad(input_modes, delta_modes):
    spec_real, spec_imag = split_complex(input_modes)
    delta_real, delta_imag = split_complex(delta_modes)
    form = "ysck,ysok->ycok"
    grad_real = jnp.einsum(form, spec_real, delta_real, precision=PRECISE) + jnp.einsum(
        form, spec_imag, delta_imag, precision=PRECISE
    )
    grad_imag = jnp.einsum(form, spec_real, delta_imag, precision=PRECISE) - jnp.einsum(
        form, spec_imag, delta_real, precision=PRECISE
    )
    return jnp.concatenate([grad_real, grad_imag], axis=-1)


def gelu_parts(value):
    normal_cdf = 0.5 * (1.0 + jax.scipy.special.erf(value * (1.0 / math.sqrt(2.0))))
    density = jnp.exp(-0.5 * value * value) * (1.0 / math.sqrt(2.0 * math.pi))
    return (value * normal_cdf, normal_cdf + value * density)


def per_device(inputs, target, spectral_weight, local_weight, bias_term):
    mode_block = spectral_weight.shape[0]
    row_count = inputs.shape[2]
    device = lax.axis_index("space")
    row_basis = row_table()
    column_basis = column_table(jnp.arange(H, dtype=jnp.int32))
    own_basis = column_table(device * row_count + jnp.arange(row_count, dtype=jnp.int32))
    mode_gain = mode_weights(device * mode_block, mode_block)[:, None, None, None]

    def to_modes(field_data):
        row_modes = row_analysis(field_data, row_basis)
        return lax.psum_scatter(
            column_modes(row_modes, own_basis), "space", scatter_dimension=0, tiled=True
        )

    def to_rows(mode_data):
        column_part = column_synth(mode_data, column_basis)
        return row_synth(
            lax.all_to_all(column_part, "space", split_axis=4, concat_axis=0, tiled=True), row_basis
        )

    input_modes = to_modes(inputs)
    mixed_modes = mix_modes(input_modes, spectral_weight) * mode_gain
    local_term = jnp.einsum(
        "co,schw->sohw", local_weight, inputs, preferred_element_type=jnp.float32
    )
    preact = to_rows(mixed_modes) + local_term + bias_term[None, :, None, None]
    activated, derivative = gelu_parts(preact)
    delta_pre = ((activated - target.astype(jnp.float32)) * derivative).astype(jnp.bfloat16)
    delta_modes = to_modes(delta_pre) * mode_gain
    grad_spectral = mix_grad(input_modes, delta_modes)
    back_modes = mix_back(delta_modes, spectral_weight)
    back_local = jnp.einsum(
        "co,sohw->schw", local_weight, delta_pre, preferred_element_type=jnp.float32
    )
    grad_input = (to_rows(back_modes) + back_local).astype(jnp.bfloat16)
    weight_term = jnp.einsum("schw,sohw->co", inputs, delta_pre, preferred_element_type=jnp.float32)
    bias_sum = jnp.sum(delta_pre, axis=(0, 2, 3), dtype=jnp.float32)
    weight_total, bias_total = lax.psum((weight_term, bias_sum), "space")
    cell_count = inputs.shape[0] * H * W
    return (grad_input, grad_spectral, weight_total / cell_count, bias_total / cell_count)


def solution(mesh):
    return jax.shard_map(
        per_device,
        mesh=mesh,
        in_specs=(
            P("dom", None, "space", None),
            P("dom", None, "space", None),
            P("space", None, None, None),
            P(),
            P(),
        ),
        out_specs=(
            P("dom", None, "space", None),
            P("space", "dom", None, None),
            P("dom", None),
            P("dom"),
        ),
        check_vma=False,
    )
```

profile of v0, /device:TPU:0, one launch (start us, length us, event | category | flops | bytes accessed | tf_op | source)
XLA Modules:
  0.0 490.5 jit_solution(4571138129678116677)
XLA Ops:
  7.2 0.0 copy-start
  7.2 0.0 reduce-scatter.3.cloned.1.call-start
  7.2 2.2 multiply_convert_fusion
  9.4 0.3 fusion.101
  9.8 0.0 copy-start.1
  9.8 10.8 %fusion.37 = f32[64,2,32,128]{3,0,2,1:T(8,128)} fusion(bf16[1,32,128,2048]{3,2,1,0:T(8,128)(2,1)} %param.5, bf16[1,64,2048]{2,1,0:T(8,128)(2,1)S(1)} %get-tuple-element.42, bf16[1,64,2048]{2,1,0:T(8,128)(2,1)S(1)} %get-tuple-element.43), kind=kOutput, calls=%fused_computation.52 | convolution fusion | flops 2148532224 | bytes 19398656 | tf_op jit(solution)/shard_map/schw,pkw->kpsch/dot_general | solution.py:38
  20.6 4.9 fusion.31
  25.5 0.3 fusion.50
  25.8 0.3 fusion.52
  26.2 1.3 pad_maximum_fusion.1
  27.5 0.0 reduce-scatter.3.cloned.1.call-update
  27.5 60.3 %reduce-scatter.3.cloned.1.call-done = f32[4,1,32,128]{3,2,0,1:T(8,128)} async-done(((f32[64,1,32,128]{3,2,0,1:T(8,128)}), f32[4,1,32,128]{3,2,0,1:T(8,128)}) %reduce-scatter.3.cloned.1.call-update) | async-done | bytes 65552 | tf_op jit(solution)/shard_map/reduce_scatter | solution.py:127
  87.8 1.0 slice_bitcast_fusion.7
  88.8 0.0 copy-done.1
  88.8 1.0 multiply_reduce_fusion.6
  89.9 0.1 maximum_multiply_fusion
  90.0 2.9 fusion.62
  92.9 2.9 fusion.69
  95.8 3.6 fusion.25
  99.4 3.2 fusion.26
  102.7 1.1 pad_maximum_fusion.2
  103.7 6.8 %copy.27 = bf16[4,2,1,32,2048]{3,0,2,1,4:T(4,128)(2,1)} copy(bf16[4,2,1,32,2048]{4,3,0,2,1:T(8,128)(2,1)} %pad_maximum_fusion.2) | data formatting | bytes 2097152 | tf_op jit(solution)/shard_map/stack | solution.py:63
  110.5 7.7 %reshape.437 = bf16[16,2,16384]{2,1,0:T(2,128)(2,1)} reshape(bf16[2048,2,1,4,32]{4,3,2,1,0:T(4,128)(2,1)} %bitcast.233) | data formatting | bytes 2097152
  118.2 4.3 all-to-all-start
  122.5 0.0 reduce-scatter.5.cloned.1.call-start
  122.6 0.0 copy-done
  122.6 0.0 copy-start.3
  122.6 22.5 %fusion.17 = f32[128,2048,32]{1,2,0:T(8,128)} fusion(bf16[32,128,2048]{2,1,0:T(8,128)(2,1)} %bitcast.229, bf16[32,32]{1,0:T(8,128)(2,1)S(1)} %copy-done), kind=kOutput, calls=%fused_computation.21 | convolution fusion | flops 536870912 | bytes 50333696 | tf_op jit(solution)/shard_map/co,schw->sohw/dot_general | solution.py:139
  145.1 0.3 all-to-all-done
  145.5 7.3 %reshape.438 = bf16[2048,2,1,4,32]{4,3,2,1,0:T(4,128)(2,1)} reshape(bf16[16,2,16384]{2,1,0:T(2,128)(2,1)} %all-to-all-done) | data formatting | bytes 2097152
  152.8 7.1 %copy.28 = bf16[4,2,1,32,16,128]{5,0,4,1,3,2:T(4,128)(2,1)} copy(bf16[4,2,1,32,16,128]{3,0,1,5,4,2:T(4,128)(2,1)} %bitcast.234) | data formatting | bytes 2097152 | tf_op jit(solution)/shard_map/all_to_all | solution.py:134
  159.9 0.0 copy-done.3
  159.9 38.7 %convert_reduce_fusion = (f32[32]{0:T(128)S(1)}, bf16[1,32,128,2048]{3,2,1,0:T(8,128)(2,1)}) fusion(bf16[1,32,128,2048]{3,2,1,0:T(8,128)(2,1)} %param.6, f32[32]{0:T(128)S(1)} %copy-done.3, f32[128,2048,32]{1,2,0:T(8,128)} %fusion.17, bf16[64,2,32,128]{3,0,1,2:T(8,128)(2,1)} %bitcast.238, bf16[1,64,2048]{2,1,0:T(8,128)(2,1)S(1)} %get-tuple-element.42, ...), kind=kOutput, calls=%fused_computation.11 | convolution fusion | flops 2290352128 | bytes 68681984 | tf_op jit(solution)/shard_map/kpsch,pkw->schw/dot_general | solution.py:42
  198.6 10.5 %fusion.40 = f32[64,2,32,128]{3,0,2,1:T(8,128)} fusion(bf16[1,32,128,2048]{3,2,1,0:T(8,128)(2,1)} %get-tuple-element.41, bf16[1,64,2048]{2,1,0:T(8,128)(2,1)S(1)} %get-tuple-element.42, bf16[1,64,2048]{2,1,0:T(8,128)(2,1)S(1)} %get-tuple-element.43), kind=kOutput, calls=%fused_computation.53 | convolution fusion | flops 2148532224 | bytes 19398656 | tf_op jit(solution)/shard_map/schw,pkw->kpsch/dot_general | solution.py:38
  209.1 4.6 fusion.34
  213.7 0.6 fusion.49
  214.3 1.3 pad_maximum_fusion.3
  215.6 0.0 reduce-scatter.5.cloned.1.call-update
  215.7 84.2 %fusion.43 = f32[32,32]{0,1:T(8,128)S(1)} fusion(bf16[32,128,2048]{2,1,0:T(8,128)(2,1)} %bitcast.230, bf16[32,128,2048]{2,1,0:T(8,128)(2,1)} %bitcast.231), kind=kOutput, calls=%fused_computation.54 | convolution fusion | flops 536870912 | bytes 33558528 | tf_op jit(solution)/shard_map/schw,sohw->co/dot_general | solution.py:152
  299.9 62.8 %all-reduce = (f32[32,32]{0,1:T(8,128)S(1)}, f32[32]{0:T(128)S(1)}) all-reduce(f32[32,32]{0,1:T(8,128)S(1)} %fusion.43, f32[32]{0:T(128)S(1)} %get-tuple-element.40), channel_id=1, replica_groups=mesh['dom'=2,'space'=16] {'space'}, use_global_device_ids=true, to_apply=%region_2.3 | all-reduce | flops 1056 | bytes 8448 | tf_op jit(solution)/shard_map/psum | solution.py:154
  362.7 0.0 reduce-scatter.5.cloned.1.call-done
  362.7 0.9 broadcast_multiply_fusion
  363.6 0.1 slice_bitcast_fusion.2
  363.7 4.3 add_bitcast_fusion
  368.0 2.9 fusion.59
  370.9 2.9 fusion.66
  373.8 3.2 fusion.23
  377.0 3.2 fusion.24
  380.3 0.1 pad_maximum_fusion.4
  380.4 5.0 %copy.34 = bf16[4,2,1,32,2048]{3,0,2,1,4:T(4,128)(2,1)} copy(bf16[4,2,1,32,2048]{4,3,0,2,1:T(8,128)(2,1)S(1)} %pad_maximum_fusion.4) | data formatting | bytes 2097152 | tf_op jit(solution)/shard_map/stack | solution.py:63
  385.4 7.6 %reshape.439 = bf16[16,2,16384]{2,1,0:T(2,128)(2,1)} reshape(bf16[2048,2,1,4,32]{4,3,2,1,0:T(4,128)(2,1)} %bitcast.235) | data formatting | bytes 2097152
  393.0 4.3 all-to-all-start.1
  397.4 0.7 copy.40
  398.0 0.5 broadcast_multiply_fusion.2
  398.6 0.0 copy-start.2
  398.6 35.7 %fusion.14 = f32[128,2048,32]{1,2,0:T(8,128)} fusion(bf16[32,128,2048]{2,1,0:T(8,128)(2,1)} %bitcast.232, bf16[32,32]{1,0:T(8,128)(2,1)S(1)} %copy-done), kind=kOutput, calls=%fused_computation.18 | convolution fusion | flops 536870912 | bytes 50333696 | tf_op jit(solution)/shard_map/co,sohw->schw/dot_general | solution.py:148
  434.2 0.0 copy-done.2
  434.2 3.6 pad_maximum_fusion
  437.8 0.0 all-to-all-done.1
  437.8 7.3 %reshape.440 = bf16[2048,2,1,4,32]{4,3,2,1,0:T(4,128)(2,1)} reshape(bf16[16,2,16384]{2,1,0:T(2,128)(2,1)} %all-to-all-done.1) | data formatting | bytes 2097152
  445.2 6.1 %copy.35 = bf16[4,2,1,32,16,128]{5,0,4,1,3,2:T(4,128)(2,1)S(1)} copy(bf16[4,2,1,32,16,128]{3,0,1,5,4,2:T(4,128)(2,1)} %bitcast.236) | data formatting | bytes 2097152 | tf_op jit(solution)/shard_map/all_to_all | solution.py:134
  451.3 31.9 %fusion.6 = bf16[1,32,128,2048]{3,2,1,0:T(8,128)(2,1)} fusion(f32[128,2048,32]{1,2,0:T(8,128)} %fusion.14, bf16[64,2,32,128]{3,0,1,2:T(8,128)(2,1)S(1)} %bitcast.237, bf16[1,64,2048]{2,1,0:T(8,128)(2,1)S(1)} %get-tuple-element.42, bf16[1,64,2048]{2,1,0:T(8,128)(2,1)S(1)} %get-tuple-element.43), kind=kOutput, calls=%fused_computation.8 | convolution fusion | flops 2164523008 | bytes 51904512 | tf_op jit(solution)/shard_map/kpsch,pkw->schw/dot_general | solution.py:42
  (6 shorter events, 0.0 us)
Async XLA Ops:
  7.2 115.4 %copy-start = (bf16[32,32]{1,0:T(8,128)(2,1)S(1)}, bf16[32,32]{1,0:T(8,128)(2,1)}, u32[]{:S(2)}) copy-start(bf16[32,32]{1,0:T(8,128)(2,1)} %param.8) | copy-start | bytes 6148
  7.2 80.6 %reduce-scatter.3.cloned.1.call-start = ((), (), s32[]{:S(2)}) async-start(), calls=%async_computation.4 | async-start | bytes 1114112 | tf_op jit(solution)/shard_map/reduce_scatter | solution.py:127
  9.8 79.0 %copy-start.1 = (f32[4,32,32,128]{3,2,1,0:T(8,128)S(1)}, f32[4,32,32,128]{3,2,1,0:T(8,128)}, u32[]{:S(2)}) copy-start(f32[4,32,32,128]{3,2,1,0:T(8,128)} %param.7) | copy-start | bytes 6291460
  118.2 27.3 %all-to-all-start = ((bf16[16,2,16384]{2,1,0:T(2,128)(2,1)}), bf16[16,2,16384]{2,1,0:T(2,128)(2,1)}, u32[]{:S(2)}, u32[]{:S(2)}) async-start(bf16[16,2,16384]{2,1,0:T(2,128)(2,1)} %reshape.437), calls=%async_computation.1 | async-start | bytes 2097152 | tf_op jit(solution)/shard_map/all_to_all | solution.py:134
  122.5 240.1 %reduce-scatter.5.cloned.1.call-start = ((), (), s32[]{:S(2)}) async-start(), calls=%async_computation.5 | async-start | bytes 1114112 | tf_op jit(solution)/shard_map/reduce_scatter | solution.py:127
  122.6 37.3 %copy-start.3 = (f32[32]{0:T(128)S(1)}, f32[32]{0:T(128)}, u32[]{:S(2)}) copy-start(f32[32]{0:T(128)} %param.9) | copy-start | bytes 388
  393.0 44.8 %all-to-all-start.1 = ((bf16[16,2,16384]{2,1,0:T(2,128)(2,1)}), bf16[16,2,16384]{2,1,0:T(2,128)(2,1)}, u32[]{:S(2)}, u32[]{:S(2)}) async-start(bf16[16,2,16384]{2,1,0:T(2,128)(2,1)} %reshape.439), calls=%async_computation.3 | async-start | bytes 2097152 | tf_op jit(solution)/shard_map/all_to_all | solution.py:134
  398.6 35.7 %copy-start.2 = (f32[4,32,32,64]{3,2,1,0:T(8,128)S(1)}, f32[4,32,32,64]{3,2,1,0:T(8,128)}, u32[]{:S(2)}) copy-start(f32[4,32,32,64]{3,2,1,0:T(8,128)} %get-tuple-element.28) | copy-start | bytes 3145732
Sparse Core Ops, SparseCore 0:
  27.6 60.1 reduce-scatter.2
  215.8 59.5 reduce-scatter.4
where the time goes:
time: 495 us; the launch traced here: 490 us
  matrix products  269 us (54%)
  blocking collectives  62.8 us (13%)
  waiting for transfers between devices  60.6 us (12%)
  local copies, waits for them, and re-layouts  56.8 us (11%)
  other arithmetic  18 us (4%)
  between operations  14.8 us (3%)
  starting transfers between devices  8.74 us (2%)
    dot_general x1, matrix products, per_device(): jnp.einsum('schw,sohw->co', inputs, delta_pre, preferred_element_type=jnp...  84.2 us
    dot_general x2, matrix products, row_synth(): jnp.einsum('kpsch,pkw->schw', spectra, basis, preferred_element_type=jnp....  70.6 us
    psum x1, blocking collectives, per_device(): weight_total, bias_total = lax.psum((weight_term, bias_sum), 'space')  62.8 us
    reduce_scatter x2, waiting for transfers between devices, to_modes(): lax.psum_scatter(column_modes(row_modes, own_basis), 'space', scatter_dim...  60.3 us
    dot_general x1, matrix products, per_device(): jnp.einsum('co,sohw->schw', local_weight, delta_pre, preferred_element_ty...  35.7 us
    unnamed x15, local copies, waits for them, and re-layouts  31.8 us
    dot_general x1, matrix products, per_device(): jnp.einsum('co,schw->sohw', local_weight, inputs, preferred_element_type=...  22.5 us
    dot_general x2, matrix products, row_analysis(): jnp.einsum('schw,pkw->kpsch', field_data, basis, preferred_element_type=j...  21.3 us
  transfers between devices with their start and end apart: 4, of which 2 were waited for; matrix products, arithmetic and copies ran while one was open for 30% of the time, Pallas kernels for 0%

commit v1 on v0

v1 whole, which is shorter than its diff:
```python
import functools
import math

import jax
import jax.numpy as jnp
from jax import lax
from jax.experimental import pallas as pl
from jax.experimental.pallas import tpu as pltpu
from jax.sharding import PartitionSpec as P

KX = 64
KY = 64
LIMIT = 56 * 1024 * 1024
F32 = jnp.float32
BF16 = jnp.bfloat16


def row_table(height, width):
    mode_index = jnp.arange(KY, dtype=jnp.int32)[:, None]
    column = jnp.arange(width, dtype=jnp.int32)[None, :]
    angles = (mode_index * column % width).astype(F32) * (2.0 * math.pi / width)
    factor = 1.0 / math.sqrt(height * width)
    return jnp.concatenate([jnp.cos(angles) * factor, -jnp.sin(angles) * factor]).astype(BF16)


def column_parts(row_index, height):
    column = jnp.arange(KX, dtype=jnp.int32)
    frequency = jnp.where(column < KX // 2, column, column + height - KX)
    angles = (row_index[:, None] * frequency[None, :] % height).astype(F32) * (2.0 * math.pi / height)
    return jnp.cos(angles), jnp.sin(angles)


def split_hi_lo(value):
    hi = value.astype(BF16)
    return hi, (value - hi.astype(F32)).astype(BF16)


def dot3(a, b_hi, b_lo):
    a_hi, a_lo = split_hi_lo(a)
    mm = functools.partial(jnp.dot, preferred_element_type=F32)
    return mm(a_hi, b_hi) + (mm(a_lo, b_hi) + mm(a_hi, b_lo))


def columns_of(row_modes, b_hi, b_lo):
    turned = row_modes.T
    half = turned.shape[0] // 2
    both = jnp.concatenate([turned[:half], turned[half:]], axis=1)
    return dot3(both, b_hi, b_lo)


def analysis_kernel(x_ref, bt_ref, bh_ref, bl_ref, out_ref):
    count, rows, width = x_ref.shape
    for c in range(count):
        row_modes = jnp.dot(x_ref[c], bt_ref[...], preferred_element_type=F32)
        out_ref[c] = columns_of(row_modes, bh_ref[...], bl_ref[...])


def analysis(x, bt, b_hi, b_lo):
    chans, rows, width = x.shape
    block = 4
    whole = lambda a: pl.BlockSpec(a.shape, lambda i: (0,) * a.ndim)
    return pl.pallas_call(
        analysis_kernel,
        grid=(chans // block,),
        in_specs=[pl.BlockSpec((block, rows, width), lambda i: (i, 0, 0)), whole(bt), whole(b_hi), whole(b_lo)],
        out_specs=pl.BlockSpec((block, KY, 2 * KX), lambda i: (i, 0, 0)),
        out_shape=jax.ShapeDtypeStruct((chans, KY, 2 * KX), F32),
        compiler_params=pltpu.CompilerParams(vmem_limit_bytes=LIMIT),
        name="analysis",
    )(x, bt, b_hi, b_lo)


def halves(value):
    half = value.shape[-1] // 2
    return value[..., :half], value[..., half:]


def cat(a, b):
    return jnp.concatenate([a, b], axis=-1)


def synth_columns(z, cb_hi, cb_lo, e_ref):
    re, im = halves(z)
    devices, _, _, rows = e_ref.shape
    both = jnp.concatenate([z, cat(im, -re)], axis=0)
    z_hi, z_lo = split_hi_lo(both)
    count = z.shape[0]
    step = max(rows, min(512, devices * rows))
    mm = functools.partial(jnp.dot, preferred_element_type=F32)
    for start in range(0, devices * rows, step):
        cols = pl.ds(start, step)
        e = mm(z_hi, cb_hi[:, cols]) + (mm(z_lo, cb_hi[:, cols]) + mm(z_hi, cb_lo[:, cols]))
        e = e.astype(BF16)
        for d in range(step // rows):
            for p in range(2):
                e_ref[start // rows + d, p] = e[p * count : (p + 1) * count, d * rows : (d + 1) * rows]


def mix_kernel(r_ref, w_ref, gain_ref, ch_ref, cl_ref, e_ref, x_ref):
    modes = w_ref.shape[0]
    parts = []
    for k in range(modes):
        x = r_ref[0, k]
        for s in range(1, r_ref.shape[0]):
            x = x + r_ref[s, k]
        x_ref[k] = x
        re, im = halves(x)
        x_rr, x_ii = cat(re, re), cat(-im, im)
        total = jnp.zeros(w_ref.shape[2:], F32)
        for c in range(w_ref.shape[1]):
            w = w_ref[k, c]
            wr, wi = halves(w)
            total = total + x_rr[c : c + 1] * w + x_ii[c : c + 1] * cat(wi, wr)
        parts.append(total * gain_ref[k])
    synth_columns(jnp.concatenate(parts, axis=0), ch_ref, cl_ref, e_ref)


def back_kernel(r_ref, w_ref, gain_ref, ch_ref, cl_ref, x_ref, e_ref, g_ref, back_ref):
    modes, chans = w_ref.shape[:2]
    for k in range(modes):
        d = r_ref[0, k]
        for s in range(1, r_ref.shape[0]):
            d = d + r_ref[s, k]
        d = d * gain_ref[k]
        dr, di = halves(d)
        d_sw = cat(di, dr)
        re, im = halves(x_ref[k])
        x_rr, x_ii = cat(re, re), cat(im, -im)
        for c in range(chans):
            g_ref[k, c] = x_rr[c : c + 1] * d + x_ii[c : c + 1] * d_sw
            wr, wi = halves(w_ref[k, c])
            term = d * cat(wr, wr) + d_sw * cat(wi, -wi)
            back_ref[pl.ds(k * chans + c, 1), :] = jnp.sum(term, axis=0, keepdims=True)
    synth_columns(back_ref[...], ch_ref, cl_ref, e_ref)


def gelu_delta(v, target):
    e = jnp.exp2(v * v * (-0.5 / math.log(2.0)))
    d = 1.0 + jnp.abs(v) * (0.3275911 / math.sqrt(2.0))
    t = pl.reciprocal(d, approx=True)
    t = t * (2.0 - d * t)
    a = (0.254829592, -0.284496736, 1.421413741, -1.453152027, 1.061405429)
    q = 0.5 * a[4]
    for coef in (a[3], a[2], a[1], a[0]):
        q = q * t + 0.5 * coef
    tail = q * t * e
    phi = jnp.where(v >= 0.0, 1.0 - tail, tail)
    slope = phi + v * e * (1.0 / math.sqrt(2.0 * math.pi))
    return (v * phi - target) * slope


def forward_kernel(x_ref, t_ref, e_ref, kron_ref, bias_ref, rb_ref, bt_ref, bh_ref, bl_ref,
                   delta_ref, modes_ref, weight_ref, rows_ref, acc_ref):
    step = pl.program_id(0)
    chans, rows, width = x_ref.shape
    flat = chans * rows
    tile = 512
    nt = (((1,), (1,)), ((), ()))

    @pl.when(step == 0)
    def _():
        acc_ref[...] = jnp.zeros_like(acc_ref)

    e = e_ref[...].reshape(flat, e_ref.shape[2])
    row_modes = jnp.zeros((flat, bt_ref.shape[1]), F32)
    for start in range(0, width, tile):
        cols = pl.ds(start, tile)
        x = x_ref[:, :, cols].reshape(flat, tile)
        v = jnp.dot(e, rb_ref[:, cols], preferred_element_type=F32)
        v = v + jnp.dot(kron_ref[...], x, preferred_element_type=F32) + bias_ref[...]
        target = t_ref[:, :, cols].reshape(flat, tile).astype(F32)
        delta = gelu_delta(v, target).astype(BF16)
        delta_ref[:, :, cols] = delta.reshape(chans, rows, tile)
        row_modes = row_modes + jnp.dot(delta, bt_ref[cols, :], preferred_element_type=F32)
        acc_ref[...] += lax.dot_general(x, delta, nt, preferred_element_type=F32)
    rows_ref[:, pl.ds(pl.multiple_of(step * rows, rows), rows), :] = row_modes.reshape(chans, rows, -1)

    @pl.when(step == pl.num_programs(0) - 1)
    def _():
        def body(o, carry):
            modes_ref[o] = columns_of(rows_ref[o], bh_ref[...], bl_ref[...])
            return carry

        lax.fori_loop(0, chans, body, 0)
        first = lax.broadcasted_iota(jnp.int32, (flat, flat), 0)
        second = lax.broadcasted_iota(jnp.int32, (flat, flat), 1)
        kept = jnp.where(first % rows == second % rows, acc_ref[...], 0.0)
        weight_ref[...] = jnp.sum(kept.reshape(chans, rows, flat), axis=1)


def forward(x, target, e, kron, bias, rb, bt, b_hi, b_lo, rows):
    chans, slab, width = x.shape
    flat = chans * rows
    whole = lambda a: pl.BlockSpec(a.shape, lambda i: (0,) * a.ndim)
    band = lambda last: pl.BlockSpec((chans, rows, last), lambda i: (0, i, 0))
    return pl.pallas_call(
        forward_kernel,
        grid=(slab // rows,),
        in_specs=[band(width), band(width), band(e.shape[2]), whole(kron), whole(bias), whole(rb), whole(bt),
                  whole(b_hi), whole(b_lo)],
        out_specs=[
            band(width),
            pl.BlockSpec((chans, KY, 2 * KX), lambda i: (0, 0, 0)),
            pl.BlockSpec((chans, flat), lambda i: (0, 0)),
        ],
        out_shape=[
            jax.ShapeDtypeStruct(x.shape, BF16),
            jax.ShapeDtypeStruct((chans, KY, 2 * KX), F32),
            jax.ShapeDtypeStruct((chans, flat), F32),
        ],
        scratch_shapes=[pltpu.VMEM((chans, slab, 2 * KY), F32), pltpu.VMEM((flat, flat), F32)],
        compiler_params=pltpu.CompilerParams(vmem_limit_bytes=LIMIT),
        name="forward",
    )(x, target, e, kron, bias, rb, bt, b_hi, b_lo)


def final_kernel(d_ref, e_ref, kron_ref, rb_ref, out_ref):
    chans, rows, width = d_ref.shape
    flat = chans * rows
    tile = 512
    e = e_ref[...].reshape(flat, e_ref.shape[2])
    for start in range(0, width, tile):
        cols = pl.ds(start, tile)
        v = jnp.dot(e, rb_ref[:, cols], preferred_element_type=F32)
        d = d_ref[:, :, cols].reshape(flat, tile)
        v = v + jnp.dot(kron_ref[...], d, preferred_element_type=F32)
        out_ref[:, :, cols] = v.astype(BF16).reshape(chans, rows, tile)


def final(delta, e, kron, rb, rows):
    chans, slab, width = delta.shape
    whole = lambda a: pl.BlockSpec(a.shape, lambda i: (0,) * a.ndim)
    band = lambda last: pl.BlockSpec((chans, rows, last), lambda i: (0, i, 0))
    return pl.pallas_call(
        final_kernel,
        grid=(slab // rows,),
        in_specs=[band(width), band(e.shape[2]), whole(kron), whole(rb)],
        out_specs=band(width),
        out_shape=jax.ShapeDtypeStruct(delta.shape, BF16),
        compiler_params=pltpu.CompilerParams(vmem_limit_bytes=LIMIT),
        name="final",
    )(delta, e, kron, rb)


def per_device(inputs, target, spectral_weight, local_weight, bias_term):
    samples, chans, slab, width = inputs.shape
    devices = lax.axis_size("space")
    height = slab * devices
    own = spectral_weight.shape[0]
    device = lax.axis_index("space")
    rows = 16

    rb = row_table(height, width)
    bt = rb.T
    rb_in = rb.reshape(2, devices, own, width).transpose(1, 0, 2, 3).reshape(2 * KY, width)
    cosines, sines = column_parts(device * slab + jnp.arange(slab, dtype=jnp.int32), height)
    b_hi, b_lo = split_hi_lo(
        jnp.concatenate([cat(cosines, -sines), cat(sines, cosines)], axis=0)
    )
    all_cos, all_sin = column_parts(jnp.arange(height, dtype=jnp.int32), height)
    c_hi, c_lo = split_hi_lo(cat(all_cos, -all_sin).T)
    mode = device * own + jnp.arange(own, dtype=jnp.int32)
    gain = jnp.broadcast_to(jnp.where(mode == 0, 1.0, 2.0).astype(F32)[:, None, None], (own, 1, 2 * KX))
    eye = jnp.eye(rows, dtype=BF16)
    kron_out = jnp.kron(local_weight.T, eye)
    kron_back = jnp.kron(local_weight, eye)
    bias = jnp.repeat(bias_term, rows)[:, None]
    params = pltpu.CompilerParams(vmem_limit_bytes=LIMIT)
    e_shape = jax.ShapeDtypeStruct((devices, 2, own * chans, slab), BF16)
    x_shape = jax.ShapeDtypeStruct((own, chans, 2 * KX), F32)

    def by_owner(modes):
        return modes.reshape(chans, devices, own, 2 * KX).transpose(1, 2, 0, 3).reshape(devices, -1)

    def to_rows(e):
        got = lax.all_to_all(e, "space", split_axis=0, concat_axis=0, tiled=True)
        got = got.reshape(devices * 2 * own, chans, slab)
        return got.transpose(1, 2, 0)

    x = inputs.reshape(chans, slab, width)
    modes = by_owner(analysis(x, bt, b_hi, b_lo))
    got = lax.all_to_all(modes, "space", split_axis=0, concat_axis=0, tiled=True)
    e, own_modes = pl.pallas_call(
        mix_kernel, out_shape=[e_shape, x_shape], compiler_params=params, name="mix"
    )(got.reshape(devices, own, chans, 2 * KX), spectral_weight, gain, c_hi, c_lo)

    delta, delta_modes, weight_part = forward(
        x, target.reshape(chans, slab, width), to_rows(e), kron_out, bias, rb_in, bt, b_hi, b_lo, rows
    )
    weight_part = weight_part.reshape(chans, chans, rows).sum(axis=-1)
    bias_part = delta_modes[:, 0, 0] * math.sqrt(height * width)
    extra = jnp.concatenate([weight_part.reshape(-1), bias_part, jnp.zeros((96,), F32)])
    extra = jnp.broadcast_to(extra[None], (devices, extra.shape[0]))
    sent = jnp.concatenate([by_owner(delta_modes), extra], axis=1)
    got = lax.all_to_all(sent, "space", split_axis=0, concat_axis=0, tiled=True)
    split = own * chans * 2 * KX
    e, grad_spectral = pl.pallas_call(
        back_kernel,
        out_shape=[e_shape, jax.ShapeDtypeStruct(spectral_weight.shape, F32)],
        scratch_shapes=[pltpu.VMEM((own * chans, 2 * KX), F32)],
        compiler_params=params,
        name="back",
    )(got[:, :split].reshape(devices, own, chans, 2 * KX), spectral_weight, gain, c_hi, c_lo, own_modes)
    totals = jnp.sum(got[:, split:], axis=0) / (samples * height * width)
    grad_local = totals[: chans * chans].reshape(chans, chans)
    grad_bias = totals[chans * chans : chans * chans + chans]
    grad_input = final(delta, to_rows(e), kron_back, rb_in, rows)
    return (grad_input.reshape(inputs.shape), grad_spectral, grad_local, grad_bias)


def solution(mesh):
    return jax.shard_map(
        per_device,
        mesh=mesh,
        in_specs=(
            P("dom", None, "space", None),
            P("dom", None, "space", None),
            P("space", None, None, None),
            P(),
            P(),
        ),
        out_specs=(
            P("dom", None, "space", None),
            P("space", "dom", None, None),
            P("dom", None),
            P("dom"),
        ),
        check_vma=False,
    )
```

time: 495 us -> 262 us (0.53)
  matrix products: 269 us -> 0 us
  Pallas kernels: 0 us -> 115 us
  blocking collectives: 62.8 us -> 35.3 us
  local copies, waits for them, and re-layouts: 56.8 us -> 33.9 us
  waiting for transfers between devices: 60.6 us -> 40.2 us
  between operations: 14.8 us -> 0.83 us
  starting transfers between devices: 8.74 us -> 17.9 us
    dot_general x17 -> x0, matrix products: 269 us -> none  [the longest x1 84.2 us: per_device(): jnp.einsum('schw,sohw->co', inputs, delta_pre, preferred_element_type=jnp...]
    pallas_call x0 -> x5, Pallas kernels: none -> 115 us  [the longest x1 70.3 us: forward(): pl.pallas_call(forward_kernel, grid=(slab // rows,), in_specs=[band(width...]
    psum x1 -> x0, blocking collectives: 62.8 us -> none  [per_device(): weight_total, bias_total = lax.psum((weight_term, bias_sum), 'space')]
    reduce_scatter x2 -> x0, waiting for transfers between devices: 60.3 us -> none  [to_modes(): lax.psum_scatter(column_modes(row_modes, own_basis), 'space', scatter_dim...]
    all_to_all x2 -> x3, waiting for transfers between devices: 0.34 us -> 40.2 us  [the longest x2 21.2 us: to_rows(): got = lax.all_to_all(e, 'space', split_axis=0, concat_axis=0, tiled=True)]
    all_to_all x0 -> x1, blocking collectives: none -> 35.3 us  [per_device(): got = lax.all_to_all(sent, 'space', split_axis=0, concat_axis=0, tiled=True)]
    unnamed x15 -> x10, local copies, waits for them, and re-layouts: 31.8 us -> 2.24 us
    mul x0 -> x2, local copies, waits for them, and re-layouts: none -> 16.8 us  [the longest x1 8.42 us: per_device(): kron_back = jnp.kron(local_weight, eye)]
  transfers between devices with their start and end apart: 4 -> 3, of which waited for: 2 -> 3; matrix products, arithmetic and copies ran while one was open for 30% -> 11% of each run, Pallas kernels for 0% -> 0%
where the time goes in v1:
time: 262 us; the launch traced here: 260 us
  Pallas kernels  115 us (44%)
  waiting for transfers between devices  40.2 us (15%)
  blocking collectives  35.3 us (13%)
  local copies, waits for them, and re-layouts  33.9 us (13%)
  starting transfers between devices  17.9 us (7%)
  other arithmetic  16.2 us (6%)
    pallas_call x1, Pallas kernels, forward(): pl.pallas_call(forward_kernel, grid=(slab // rows,), in_specs=[band(width...  70.3 us
    all_to_all x1, blocking collectives, per_device(): got = lax.all_to_all(sent, 'space', split_axis=0, concat_axis=0, tiled=True)  35.3 us
    all_to_all x2, waiting for transfers between devices, to_rows(): got = lax.all_to_all(e, 'space', split_axis=0, concat_axis=0, tiled=True)  21.2 us
    pallas_call x1, Pallas kernels, final(): pl.pallas_call(final_kernel, grid=(slab // rows,), in_specs=[band(width),...  19.7 us
    all_to_all x1, waiting for transfers between devices, per_device(): lax.all_to_all(modes, 'space', split_axis=0, concat_axis=0, tiled=True)  19 us
    pallas_call x1, Pallas kernels, analysis(): pl.pallas_call(analysis_kernel, grid=(chans // block,), in_specs=[pl.Bloc...  15.3 us
    all_to_all x2, starting transfers between devices, to_rows(): got = lax.all_to_all(e, 'space', split_axis=0, concat_axis=0, tiled=True)  10.5 us
    mul x1, local copies, waits for them, and re-layouts, per_device(): kron_back = jnp.kron(local_weight, eye)  8.42 us
  transfers between devices with their start and end apart: 3, of which 3 were waited for; matrix products, arithmetic and copies ran while one was open for 11% of the time, Pallas kernels for 0%

profile of v1, /device:TPU:0, one launch (start us, length us, event | category | flops | bytes accessed | tf_op | source)
XLA Modules:
  0.0 259.5 jit_solution(8510975462389478968)
XLA Ops:
  0.7 0.3 fusion.19
  1.0 0.7 subtract_convert_fusion.1.bl_ref
  1.8 0.7 fusion.16.bh_ref
  2.5 0.2 fusion.2
  2.7 0.3 copy.41
  3.0 3.9 %cosine_multiply_fusion = (bf16[64,2048]{0,1:T(8,128)(2,1)S(1)}, bf16[64,2048]{0,1:T(8,128)(2,1)S(1)}) fusion(f32[64,2048]{0,1:T(8,128)S(1)} %copy.41), kind=kLoop, calls=%fused_computation.10 | loop fusion | flops 786432 | bytes 1048576 | tf_op jit(solution)/shard_map/mul | solution.py:23
  6.9 1.1 fusion.21.bt_ref
  8.0 15.3 %analysis.1 = f32[32,64,128]{2,1,0:T(8,128)} custom-call(bf16[32,128,2048]{2,1,0:T(8,128)(2,1)} %bitcast.45, bf16[2048,128]{1,0:T(8,128)(2,1)} %fusion.21.bt_ref, bf16[256,128]{1,0:T(8,128)(2,1)} %fusion.16.bh_ref, bf16[256,128]{1,0:T(8,128)(2,1)} %subtract_convert_fusion.1.bl_ref), custom_call_target="tpu_custom_call" | custom-call | tf_op jit(solution)/shard_map/analysis/pallas_call | solution.py:62
  23.3 2.8 %copy.42 = f32[16,4,32,128]{3,2,1,0:T(8,128)} copy(f32[16,4,32,128]{3,1,0,2:T(4,128)} %bitcast.53) | data formatting | bytes 2097152 | tf_op jit(solution)/shard_map/transpose | solution.py:273
  26.1 7.4 %all-to-all-start = ((f32[16,1,16384]{2,1,0:T(1,128)}), f32[16,1,16384]{2,1,0:T(1,128)S(1)}, u32[]{:S(2)}, u32[]{:S(2)}) async-start(f32[16,1,16384]{2,1,0:T(1,128)} %bitcast.5), calls=%async_computation | async-start | bytes 2097152 | tf_op jit(solution)/shard_map/all_to_all | solution.py:282
  33.5 2.1 fusion.12
  35.7 0.9 subtract_convert_fusion.cl_ref
  36.5 0.0 copy-start.1
  36.5 0.0 copy-start.2
  36.5 0.9 fusion.ch_ref
  37.4 19.0 %all-to-all-done = f32[16,1,16384]{2,1,0:T(1,128)S(1)} async-done(((f32[16,1,16384]{2,1,0:T(1,128)}), f32[16,1,16384]{2,1,0:T(1,128)S(1)}, u32[]{:S(2)}, u32[]{:S(2)}) %all-to-all-start) | async-done | bytes 1048608 | tf_op jit(solution)/shard_map/all_to_all | solution.py:282
  56.5 0.0 copy-start
  56.5 0.7 broadcast_in_dim.40.gain_ref
  57.2 0.2 copy-done
  57.4 4.7 %mix.1 = (bf16[16,2,128,128]{3,2,1,0:T(8,128)(2,1)}, f32[4,32,128]{2,1,0:T(8,128)}) custom-call(f32[16,4,32,128]{3,2,1,0:T(8,128)} %bitcast.58, f32[4,32,32,128]{3,2,1,0:T(8,128)} %w_ref.3, f32[4,1,128]{2,1,0:T(1,128)} %broadcast_in_dim.40.gain_ref, bf16[128,2048]{1,0:T(8,128)(2,1)} %fusion.ch_ref, bf16[128,2048]{1,0:T(8,128)(2,1)} %subtract_convert_fusion.cl_ref), custom_call_target="tpu_custom_call" | custom-call | tf_op jit(solution)/shard_map/mix/pallas_call | solution.py:283
  62.2 6.9 %all-to-all-start.1 = ((bf16[16,2,128,128]{3,2,1,0:T(8,128)(2,1)}), bf16[16,2,128,128]{3,2,1,0:T(8,128)(2,1)S(1)}, u32[]{:S(2)}, u32[]{:S(2)}) async-start(bf16[16,2,128,128]{3,2,1,0:T(8,128)(2,1)} %get-tuple-element.11), calls=%async_computation.1 | async-start | bytes 2097152 | tf_op jit(solution)/shard_map/all_to_all | solution.py:276
  69.1 0.0 copy-done.1
  69.1 0.1 copy.44
  69.1 0.0 copy-done.2
  69.1 0.1 broadcast_in_dim.41
  69.2 0.9 broadcast_in_dim_reshape.4.bias_ref
  70.1 0.3 maximum_convert_fusion
  70.4 0.2 copy.45
  70.6 0.2 convert_element_type.58
  70.8 0.2 copy.46
  71.0 0.9 reshape.110.rb_ref
  72.0 3.7 %broadcast_multiply_fusion = (bf16[32,16,32,16]{3,2,1,0:T(8,128)(2,1)}, bf16[32,16,32,16]{3,2,1,0:T(8,128)(2,1)}) fusion(bf16[32,32]{1,0:T(8,128)(2,1)S(1)} %copy-done.1, bf16[16,16]{1,0:T(8,128)(2,1)S(1)} %fusion.20, bf16[32,32]{1,0:T(8,128)(2,1)S(1)} %copy.44), kind=kLoop, calls=%fused_computation | loop fusion | flops 524288 | bytes 1053184 | tf_op jit(solution)/shard_map/jit(kron)/mul | solution.py:266
  75.6 8.4 %mul.157.kron_ref = bf16[512,512]{1,0:T(8,128)(2,1)} reshape(bf16[32,16,32,16]{3,2,1,0:T(8,128)(2,1)} %get-tuple-element.21) | data formatting | bytes 1048576 | tf_op jit(solution)/shard_map/jit(kron)/mul | solution.py:265
  84.0 7.9 %all-to-all-done.1 = bf16[16,2,128,128]{3,2,1,0:T(8,128)(2,1)S(1)} async-done(((bf16[16,2,128,128]{3,2,1,0:T(8,128)(2,1)}), bf16[16,2,128,128]{3,2,1,0:T(8,128)(2,1)S(1)}, u32[]{:S(2)}, u32[]{:S(2)}) %all-to-all-start.1) | async-done | bytes 1048608 | tf_op jit(solution)/shard_map/all_to_all | solution.py:276
  92.0 1.7 copy.43
  93.7 70.3 %forward.1 = (bf16[32,128,2048]{2,1,0:T(8,128)(2,1)}, f32[32,64,128]{2,1,0:T(8,128)}, f32[32,512]{1,0:T(8,128)}) custom-call(bf16[32,128,2048]{2,1,0:T(8,128)(2,1)} %bitcast.46, bf16[32,128,2048]{2,1,0:T(8,128)(2,1)} %bitcast.47, bf16[32,128,128]{2,1,0:T(8,128)(2,1)} %bitcast.51, bf16[512,512]{1,0:T(8,128)(2,1)} %mul.157.kron_ref, ...), custom_call_target="tpu_custom_call" | custom-call | tf_op jit(solution)/shard_map/forward/pallas_call | solution.py:196
  164.0 1.2 multiply_reduce_fusion
  165.2 1.0 copy.49
  166.2 0.1 copy.50
  166.3 0.1 reshape.114
  166.4 1.8 copy.48
  168.2 0.6 copy.58
  168.8 0.1 concatenate.26
  168.9 0.1 pad_maximum_fusion
  169.0 0.8 all_to_all.23
  169.8 35.3 %all_to_all.31 = f32[16,1,17536]{2,1,0:T(1,128)S(1)} all-to-all(f32[16,1,17536]{2,1,0:T(1,128)S(1)} %all_to_all.23), channel_id=1, replica_groups=mesh['dom'=2,'space'=16] {'space'}, dimensions={0} | all-to-all | bytes 2244608 | tf_op jit(solution)/shard_map/all_to_all | solution.py:295
  205.1 0.1 copy.57
  205.2 0.1 slice_bitcast_fusion
  205.3 1.2 copy.54
  206.5 5.1 %back.1 = (bf16[16,2,128,128]{3,2,1,0:T(8,128)(2,1)}, f32[4,32,32,128]{3,2,1,0:T(8,128)}) custom-call(f32[16,4,32,128]{3,2,1,0:T(8,128)} %bitcast.59, f32[4,32,32,128]{3,2,1,0:T(8,128)} %w_ref.3, f32[4,1,128]{2,1,0:T(1,128)} %broadcast_in_dim.40.gain_ref, bf16[128,2048]{1,0:T(8,128)(2,1)} %fusion.ch_ref, bf16[128,2048]{1,0:T(8,128)(2,1)} %subtract_convert_fusion.cl_ref, ...), custom_call_target="tpu_custom_call" | custom-call | tf_op jit(solution)/shard_map/back/pallas_call | solution.py:297
  211.6 3.7 %all-to-all-start.3 = ((bf16[16,2,128,128]{3,2,1,0:T(8,128)(2,1)}), bf16[16,2,128,128]{3,2,1,0:T(8,128)(2,1)S(1)}, u32[]{:S(2)}, u32[]{:S(2)}) async-start(bf16[16,2,128,128]{3,2,1,0:T(8,128)(2,1)} %get-tuple-element.16), calls=%async_computation.3 | async-start | bytes 2097152 | tf_op jit(solution)/shard_map/all_to_all | solution.py:276
  215.3 8.4 %mul.163.kron_ref = bf16[512,512]{1,0:T(8,128)(2,1)} reshape(bf16[32,16,32,16]{3,2,1,0:T(8,128)(2,1)} %get-tuple-element.20) | data formatting | bytes 1048576 | tf_op jit(solution)/shard_map/jit(kron)/mul | solution.py:266
  223.7 0.5 slice.28
  224.2 0.7 slice.23
  224.9 13.2 %all-to-all-done.3 = bf16[16,2,128,128]{3,2,1,0:T(8,128)(2,1)S(1)} async-done(((bf16[16,2,128,128]{3,2,1,0:T(8,128)(2,1)}), bf16[16,2,128,128]{3,2,1,0:T(8,128)(2,1)S(1)}, u32[]{:S(2)}, u32[]{:S(2)}) %all-to-all-start.3) | async-done | bytes 1048608 | tf_op jit(solution)/shard_map/all_to_all | solution.py:276
  238.2 1.7 copy.51
  239.8 19.7 %final.1 = bf16[32,128,2048]{2,1,0:T(8,128)(2,1)} custom-call(bf16[32,128,2048]{2,1,0:T(8,128)(2,1)} %get-tuple-element.12.d_ref, bf16[32,128,128]{2,1,0:T(8,128)(2,1)} %bitcast.52, bf16[512,512]{1,0:T(8,128)(2,1)} %mul.163.kron_ref, bf16[128,2048]{1,0:T(8,128)(2,1)} %reshape.110.rb_ref), custom_call_target="tpu_custom_call" | custom-call | tf_op jit(solution)/shard_map/final/pallas_call | solution.py:234
  (10 shorter events, 0.1 us)
Async XLA Ops:
  26.1 30.3 %all-to-all-start = ((f32[16,1,16384]{2,1,0:T(1,128)}), f32[16,1,16384]{2,1,0:T(1,128)S(1)}, u32[]{:S(2)}, u32[]{:S(2)}) async-start(f32[16,1,16384]{2,1,0:T(1,128)} %bitcast.5), calls=%async_computation | async-start | bytes 2097152 | tf_op jit(solution)/shard_map/all_to_all | solution.py:282
  36.5 32.5 %copy-start.1 = (bf16[32,32]{1,0:T(8,128)(2,1)S(1)}, bf16[32,32]{1,0:T(8,128)(2,1)}, u32[]{:S(2)}) copy-start(bf16[32,32]{1,0:T(8,128)(2,1)} %param.8) | copy-start | bytes 6148
  36.5 32.6 %copy-start.2 = (f32[32]{0:T(128)S(1)}, f32[32]{0:T(128)}, u32[]{:S(2)}) copy-start(f32[32]{0:T(128)} %param.9) | copy-start | bytes 388
  56.5 1.0 copy-start
  62.2 29.8 %all-to-all-start.1 = ((bf16[16,2,128,128]{3,2,1,0:T(8,128)(2,1)}), bf16[16,2,128,128]{3,2,1,0:T(8,128)(2,1)S(1)}, u32[]{:S(2)}, u32[]{:S(2)}) async-start(bf16[16,2,128,128]{3,2,1,0:T(8,128)(2,1)} %get-tuple-element.11), calls=%async_computation.1 | async-start | bytes 2097152 | tf_op jit(solution)/shard_map/all_to_all | solution.py:276
  211.6 26.6 %all-to-all-start.3 = ((bf16[16,2,128,128]{3,2,1,0:T(8,128)(2,1)}), bf16[16,2,128,128]{3,2,1,0:T(8,128)(2,1)S(1)}, u32[]{:S(2)}, u32[]{:S(2)}) async-start(bf16[16,2,128,128]{3,2,1,0:T(8,128)(2,1)} %get-tuple-element.16), calls=%async_computation.3 | async-start | bytes 2097152 | tf_op jit(solution)/shard_map/all_to_all | solution.py:276

commit v2 on v1

--- a/solution.py
+++ b/solution.py
@@ -3,6 +3,8 @@
 
 import jax
 import jax.numpy as jnp
+import ml_dtypes
+import numpy as np
 from jax import lax
 from jax.experimental import pallas as pl
 from jax.experimental.pallas import tpu as pltpu
@@ -16,11 +18,26 @@
 
 
 def row_table(height, width):
-    mode_index = jnp.arange(KY, dtype=jnp.int32)[:, None]
-    column = jnp.arange(width, dtype=jnp.int32)[None, :]
-    angles = (mode_index * column % width).astype(F32) * (2.0 * math.pi / width)
+    angles = (np.arange(KY)[:, None] * np.arange(width)[None, :] % width) * (2.0 * math.pi / width)
     factor = 1.0 / math.sqrt(height * width)
-    return jnp.concatenate([jnp.cos(angles) * factor, -jnp.sin(angles) * factor]).astype(BF16)
+    return np.concatenate([np.cos(angles) * factor, -np.sin(angles) * factor]).astype(ml_dtypes.bfloat16)
+
+
+def column_table(height):
+    column = np.arange(KX)
+    frequency = np.where(column < KX // 2, column, column + height - KX)
+    angles = (frequency[:, None] * np.arange(height)[None, :] % height) * (2.0 * math.pi / height)
+    table = np.concatenate([np.cos(angles), -np.sin(angles)]).astype(np.float32)
+    hi = table.astype(ml_dtypes.bfloat16)
+    return hi, (table - hi.astype(np.float32)).astype(ml_dtypes.bfloat16)
+
+
+def spread(weight, rows):
+    flat = weight.shape[0] * rows
+    place = jnp.arange(flat, dtype=jnp.int32)
+    chosen = (place[:, None] // rows == jnp.arange(weight.shape[0])[None, :]).astype(BF16)
+    wide = jnp.dot(jnp.dot(chosen, weight), chosen.T)
+    return jnp.where(place[:, None] % rows == place[None, :] % rows, wide, 0.0).astype(BF16)
 
 
 def column_parts(row_index, height):
@@ -50,9 +67,10 @@
 
 def analysis_kernel(x_ref, bt_ref, bh_ref, bl_ref, out_ref):
     count, rows, width = x_ref.shape
+    flat = x_ref[...].reshape(count * rows, width)
+    row_modes = jnp.dot(flat, bt_ref[...], preferred_element_type=F32)
     for c in range(count):
-        row_modes = jnp.dot(x_ref[c], bt_ref[...], preferred_element_type=F32)
-        out_ref[c] = columns_of(row_modes, bh_ref[...], bl_ref[...])
+        out_ref[c] = columns_of(row_modes[c * rows : (c + 1) * rows], bh_ref[...], bl_ref[...])
 
 
 def analysis(x, bt, b_hi, b_lo):
@@ -251,19 +269,17 @@
     rows = 16
 
     rb = row_table(height, width)
-    bt = rb.T
-    rb_in = rb.reshape(2, devices, own, width).transpose(1, 0, 2, 3).reshape(2 * KY, width)
+    bt = jnp.asarray(np.ascontiguousarray(rb.T))
+    rb_in = jnp.asarray(rb.reshape(2, devices, own, width).transpose(1, 0, 2, 3).reshape(2 * KY, width))
     cosines, sines = column_parts(device * slab + jnp.arange(slab, dtype=jnp.int32), height)
     b_hi, b_lo = split_hi_lo(
         jnp.concatenate([cat(cosines, -sines), cat(sines, cosines)], axis=0)
     )
-    all_cos, all_sin = column_parts(jnp.arange(height, dtype=jnp.int32), height)
-    c_hi, c_lo = split_hi_lo(cat(all_cos, -all_sin).T)
+    c_hi, c_lo = (jnp.asarray(table) for table in column_table(height))
     mode = device * own + jnp.arange(own, dtype=jnp.int32)
     gain = jnp.broadcast_to(jnp.where(mode == 0, 1.0, 2.0).astype(F32)[:, None, None], (own, 1, 2 * KX))
-    eye = jnp.eye(rows, dtype=BF16)
-    kron_out = jnp.kron(local_weight.T, eye)
-    kron_back = jnp.kron(local_weight, eye)
+    kron_out = spread(local_weight.T, rows)
+    kron_back = spread(local_weight, rows)
     bias = jnp.repeat(bias_term, rows)[:, None]
     params = pltpu.CompilerParams(vmem_limit_bytes=LIMIT)
     e_shape = jax.ShapeDtypeStruct((devices, 2, own * chans, slab), BF16)
@@ -289,19 +305,18 @@
     )
     weight_part = weight_part.reshape(chans, chans, rows).sum(axis=-1)
     bias_part = delta_modes[:, 0, 0] * math.sqrt(height * width)
-    extra = jnp.concatenate([weight_part.reshape(-1), bias_part, jnp.zeros((96,), F32)])
+    extra = jnp.concatenate([weight_part.reshape(-1), bias_part, jnp.zeros((992,), F32)])
     extra = jnp.broadcast_to(extra[None], (devices, extra.shape[0]))
-    sent = jnp.concatenate([by_owner(delta_modes), extra], axis=1)
-    got = lax.all_to_all(sent, "space", split_axis=0, concat_axis=0, tiled=True)
-    split = own * chans * 2 * KX
+    got = lax.all_to_all(by_owner(delta_modes), "space", split_axis=0, concat_axis=0, tiled=True)
+    terms = lax.all_to_all(extra, "space", split_axis=0, concat_axis=0, tiled=True)
     e, grad_spectral = pl.pallas_call(
         back_kernel,
         out_shape=[e_shape, jax.ShapeDtypeStruct(spectral_weight.shape, F32)],
         scratch_shapes=[pltpu.VMEM((own * chans, 2 * KX), F32)],
         compiler_params=params,
         name="back",
-    )(got[:, :split].reshape(devices, own, chans, 2 * KX), spectral_weight, gain, c_hi, c_lo, own_modes)
-    totals = jnp.sum(got[:, split:], axis=0) / (samples * height * width)
+    )(got.reshape(devices, own, chans, 2 * KX), spectral_weight, gain, c_hi, c_lo, own_modes)
+    totals = jnp.sum(terms, axis=0) / (samples * height * width)
     grad_local = totals[: chans * chans].reshape(chans, chans)
     grad_bias = totals[chans * chans : chans * chans + chans]
     grad_input = final(delta, to_rows(e), kron_back, rb_in, rows)

time: 262 us -> 255 us (0.973)
  waiting for transfers between devices: 40.2 us -> 87 us
  blocking collectives: 35.3 us -> 0 us
  local copies, waits for them, and re-layouts: 33.9 us -> 14.1 us
  starting transfers between devices: 17.9 us -> 31.6 us
  other arithmetic: 16.2 us -> 3.19 us
  matrix products: 0 us -> 2.75 us
    all_to_all x1 -> x0, blocking collectives: 35.3 us -> none  [per_device(): got = lax.all_to_all(sent, 'space', split_axis=0, concat_axis=0, tiled=True)]
    all_to_all x0 -> x2, waiting for transfers between devices: none -> 23.3 us  [the longest x1 20.5 us: per_device(): lax.all_to_all(by_owner(delta_modes), 'space', split_axis=0, concat_axis=...]
    all_to_all x2, waiting for transfers between devices: 21.2 us -> 40.8 us  [to_rows(): got = lax.all_to_all(e, 'space', split_axis=0, concat_axis=0, tiled=True)]
    mul x2 -> x0, local copies, waits for them, and re-layouts: 16.8 us -> none  [the longest x1 8.42 us: per_device(): kron_back = jnp.kron(local_weight, eye)]
    all_to_all x0 -> x2, starting transfers between devices: none -> 13.7 us  [the longest x1 6.87 us: per_device(): lax.all_to_all(by_owner(delta_modes), 'space', split_axis=0, concat_axis=...]
    mul x2 -> x0, other arithmetic: 7.53 us -> none  [the longest x1 3.87 us: row_table(): jnp.cos(angles) * factor]
    all_to_all x1, waiting for transfers between devices: 19 us -> 22.9 us  [per_device(): lax.all_to_all(modes, 'space', split_axis=0, concat_axis=0, tiled=True)]
    dot_general x0 -> x2, matrix products: none -> 2.75 us  [spread(): wide = jnp.dot(jnp.dot(chosen, weight), chosen.T)]
  transfers between devices with their start and end apart: 3 -> 5, of which waited for: 3 -> 5; matrix products, arithmetic and copies ran while one was open for 11% -> 3% of each run, Pallas kernels for 0% -> 2%
where the time goes in v2:
time: 255 us; the launch traced here: 253 us
  Pallas kernels  113 us (44%)
  waiting for transfers between devices  87 us (34%)
  starting transfers between devices  31.6 us (12%)
  local copies, waits for them, and re-layouts  14.1 us (6%)
  other arithmetic  3.19 us (1%)
  matrix products  2.75 us (1%)
    pallas_call x1, Pallas kernels, forward(): pl.pallas_call(forward_kernel, grid=(slab // rows,), in_specs=[band(width...  70.4 us
    all_to_all x2, waiting for transfers between devices, to_rows(): got = lax.all_to_all(e, 'space', split_axis=0, concat_axis=0, tiled=True)  40.8 us
    all_to_all x1, waiting for transfers between devices, per_device(): lax.all_to_all(modes, 'space', split_axis=0, concat_axis=0, tiled=True)  22.9 us
    all_to_all x1, waiting for transfers between devices, per_device(): lax.all_to_all(by_owner(delta_modes), 'space', split_axis=0, concat_axis=...  20.5 us
    pallas_call x1, Pallas kernels, final(): pl.pallas_call(final_kernel, grid=(slab // rows,), in_specs=[band(width),...  19.7 us
    pallas_call x1, Pallas kernels, analysis(): pl.pallas_call(analysis_kernel, grid=(chans // block,), in_specs=[pl.Bloc...  13.1 us
    all_to_all x2, starting transfers between devices, to_rows(): got = lax.all_to_all(e, 'space', split_axis=0, concat_axis=0, tiled=True)  10.5 us
    all_to_all x1, starting transfers between devices, per_device(): lax.all_to_all(modes, 'space', split_axis=0, concat_axis=0, tiled=True)  7.38 us
  transfers between devices with their start and end apart: 5, of which 5 were waited for; matrix products, arithmetic and copies ran while one was open for 3% of the time, Pallas kernels for 2%

profile of v2, /device:TPU:0, one launch (start us, length us, event | category | flops | bytes accessed | tf_op | source)
XLA Modules:
  0.0 252.6 jit_solution(1472377615332245770)
XLA Ops:
  0.6 0.0 copy-start
  0.6 0.0 copy-start.3
  0.7 0.3 fusion.14
  1.0 0.7 subtract_convert_fusion.bl_ref
  1.8 0.7 fusion.11.bh_ref
  2.5 13.1 %analysis.1 = f32[32,64,128]{2,1,0:T(8,128)} custom-call(bf16[32,128,2048]{2,1,0:T(8,128)(2,1)} %bitcast.21, bf16[2048,128]{1,0:T(8,128)(2,1)} %constant.101.clone.bt_ref, bf16[256,128]{1,0:T(8,128)(2,1)} %fusion.11.bh_ref, bf16[256,128]{1,0:T(8,128)(2,1)} %subtract_convert_fusion.bl_ref), custom_call_target="tpu_custom_call" | custom-call | tf_op jit(solution)/shard_map/analysis/pallas_call | solution.py:80
  15.6 2.8 %copy.41 = f32[16,4,32,128]{3,2,1,0:T(8,128)} copy(f32[16,4,32,128]{3,1,0,2:T(4,128)} %bitcast.27) | data formatting | bytes 2097152 | tf_op jit(solution)/shard_map/transpose | solution.py:289
  18.4 7.4 %all-to-all-start = ((f32[16,1,16384]{2,1,0:T(1,128)}), f32[16,1,16384]{2,1,0:T(1,128)S(1)}, u32[]{:S(2)}, u32[]{:S(2)}) async-start(f32[16,1,16384]{2,1,0:T(1,128)} %bitcast.4), calls=%async_computation | async-start | bytes 2097152 | tf_op jit(solution)/shard_map/all_to_all | solution.py:298
  25.8 22.9 %all-to-all-done = f32[16,1,16384]{2,1,0:T(1,128)S(1)} async-done(((f32[16,1,16384]{2,1,0:T(1,128)}), f32[16,1,16384]{2,1,0:T(1,128)S(1)}, u32[]{:S(2)}, u32[]{:S(2)}) %all-to-all-start) | async-done | bytes 1048608 | tf_op jit(solution)/shard_map/all_to_all | solution.py:298
  48.7 0.0 copy-start.2
  48.7 0.7 broadcast_in_dim.23.gain_ref
  49.5 0.2 copy-done.2
  49.7 4.7 %mix.1 = (bf16[16,2,128,128]{3,2,1,0:T(8,128)(2,1)}, f32[4,32,128]{2,1,0:T(8,128)}) custom-call(f32[16,4,32,128]{3,2,1,0:T(8,128)} %bitcast.31, f32[4,32,32,128]{3,2,1,0:T(8,128)} %w_ref.3, f32[4,1,128]{2,1,0:T(1,128)} %broadcast_in_dim.23.gain_ref, bf16[128,2048]{1,0:T(8,128)(2,1)} %constant.103.clone.ch_ref, bf16[128,2048]{1,0:T(8,128)(2,1)} %constant.104.clone.cl_ref), custom_call_target="tpu_custom_call" | custom-call | tf_op jit(solution)/shard_map/mix/pallas_call | solution.py:299
  54.5 6.9 %all-to-all-start.1 = ((bf16[16,2,128,128]{3,2,1,0:T(8,128)(2,1)}), bf16[16,2,128,128]{3,2,1,0:T(8,128)(2,1)S(1)}, u32[]{:S(2)}, u32[]{:S(2)}) async-start(bf16[16,2,128,128]{3,2,1,0:T(8,128)(2,1)} %get-tuple-element.11), calls=%async_computation.1 | async-start | bytes 2097152 | tf_op jit(solution)/shard_map/all_to_all | solution.py:292
  61.3 0.0 copy-done.3
  61.3 0.1 broadcast_in_dim.25
  61.4 0.9 broadcast_in_dim_reshape.4.bias_ref
  62.3 0.0 copy-done
  62.3 1.4 compare_select_fusion.1.kron_ref
  63.6 20.6 %all-to-all-done.1 = bf16[16,2,128,128]{3,2,1,0:T(8,128)(2,1)S(1)} async-done(((bf16[16,2,128,128]{3,2,1,0:T(8,128)(2,1)}), bf16[16,2,128,128]{3,2,1,0:T(8,128)(2,1)S(1)}, u32[]{:S(2)}, u32[]{:S(2)}) %all-to-all-start.1) | async-done | bytes 1048608 | tf_op jit(solution)/shard_map/all_to_all | solution.py:292
  84.3 1.7 copy.42
  86.0 70.4 %forward.1 = (bf16[32,128,2048]{2,1,0:T(8,128)(2,1)}, f32[32,64,128]{2,1,0:T(8,128)}, f32[32,512]{1,0:T(8,128)}) custom-call(bf16[32,128,2048]{2,1,0:T(8,128)(2,1)} %bitcast.22, bf16[32,128,2048]{2,1,0:T(8,128)(2,1)} %bitcast.23, bf16[32,128,128]{2,1,0:T(8,128)(2,1)} %bitcast.25, bf16[512,512]{1,0:T(8,128)(2,1)} %compare_select_fusion.1.kron_ref, ...), custom_call_target="tpu_custom_call" | custom-call | tf_op jit(solution)/shard_map/forward/pallas_call | solution.py:214
  156.4 2.8 %copy.44 = f32[16,4,32,128]{3,2,1,0:T(8,128)} copy(f32[16,4,32,128]{3,1,0,2:T(4,128)} %bitcast.32) | data formatting | bytes 2097152 | tf_op jit(solution)/shard_map/transpose | solution.py:289
  159.2 6.9 %all-to-all-start.2 = ((f32[16,1,16384]{2,1,0:T(1,128)}), f32[16,1,16384]{2,1,0:T(1,128)S(1)}, u32[]{:S(2)}, u32[]{:S(2)}) async-start(f32[16,1,16384]{2,1,0:T(1,128)} %bitcast.10), calls=%async_computation.2 | async-start | bytes 2097152 | tf_op jit(solution)/shard_map/all_to_all | solution.py:310
  166.1 1.0 copy.46
  167.1 0.1 copy.47
  167.2 0.1 reshape.162
  167.2 1.2 multiply_reduce_fusion
  168.5 0.1 concatenate.15
  168.6 20.5 %all-to-all-done.2 = f32[16,1,16384]{2,1,0:T(1,128)S(1)} async-done(((f32[16,1,16384]{2,1,0:T(1,128)}), f32[16,1,16384]{2,1,0:T(1,128)S(1)}, u32[]{:S(2)}, u32[]{:S(2)}) %all-to-all-start.2) | async-done | bytes 1048608 | tf_op jit(solution)/shard_map/all_to_all | solution.py:310
  189.0 0.0 copy-start.1
  189.0 0.8 broadcast_in_dim.47
  189.8 6.9 %all-to-all-start.4 = ((f32[16,1,2048]{2,1,0:T(1,128)}), f32[16,1,2048]{2,1,0:T(1,128)S(1)}, u32[]{:S(2)}, u32[]{:S(2)}) async-start(f32[16,1,2048]{2,1,0:T(1,128)} %broadcast_in_dim.47), calls=%async_computation.4 | async-start | bytes 262144 | tf_op jit(solution)/shard_map/all_to_all | solution.py:311
  196.7 0.0 copy-done.1
  196.7 5.1 %back.1 = (bf16[16,2,128,128]{3,2,1,0:T(8,128)(2,1)}, f32[4,32,32,128]{3,2,1,0:T(8,128)}) custom-call(f32[16,4,32,128]{3,2,1,0:T(8,128)} %bitcast.30, f32[4,32,32,128]{3,2,1,0:T(8,128)} %w_ref.3, f32[4,1,128]{2,1,0:T(1,128)} %broadcast_in_dim.23.gain_ref, bf16[128,2048]{1,0:T(8,128)(2,1)} %constant.103.clone.ch_ref, ...), custom_call_target="tpu_custom_call" | custom-call | tf_op jit(solution)/shard_map/back/pallas_call | solution.py:312
  201.8 2.8 %all-to-all-done.4 = f32[16,1,2048]{2,1,0:T(1,128)S(1)} async-done(((f32[16,1,2048]{2,1,0:T(1,128)}), f32[16,1,2048]{2,1,0:T(1,128)S(1)}, u32[]{:S(2)}, u32[]{:S(2)}) %all-to-all-start.4) | async-done | bytes 131104 | tf_op jit(solution)/shard_map/all_to_all | solution.py:311
  204.6 3.7 %all-to-all-start.3 = ((bf16[16,2,128,128]{3,2,1,0:T(8,128)(2,1)}), bf16[16,2,128,128]{3,2,1,0:T(8,128)(2,1)S(1)}, u32[]{:S(2)}, u32[]{:S(2)}) async-start(bf16[16,2,128,128]{3,2,1,0:T(8,128)(2,1)} %get-tuple-element.15), calls=%async_computation.3 | async-start | bytes 2097152 | tf_op jit(solution)/shard_map/all_to_all | solution.py:292
  208.3 1.4 compare_select_fusion.kron_ref
  209.7 0.1 reduce_sum.19
  209.8 0.5 slice.18
  210.3 0.7 slice.15
  211.0 20.2 %all-to-all-done.3 = bf16[16,2,128,128]{3,2,1,0:T(8,128)(2,1)S(1)} async-done(((bf16[16,2,128,128]{3,2,1,0:T(8,128)(2,1)}), bf16[16,2,128,128]{3,2,1,0:T(8,128)(2,1)S(1)}, u32[]{:S(2)}, u32[]{:S(2)}) %all-to-all-start.3) | async-done | bytes 1048608 | tf_op jit(solution)/shard_map/all_to_all | solution.py:292
  231.2 1.7 copy.45
  232.9 19.7 %final.1 = bf16[32,128,2048]{2,1,0:T(8,128)(2,1)} custom-call(bf16[32,128,2048]{2,1,0:T(8,128)(2,1)} %get-tuple-element.12.d_ref, bf16[32,128,128]{2,1,0:T(8,128)(2,1)} %bitcast.26, bf16[512,512]{1,0:T(8,128)(2,1)} %compare_select_fusion.kron_ref, bf16[128,2048]{1,0:T(8,128)(2,1)} %constant.102.clone.rb_ref), custom_call_target="tpu_custom_call" | custom-call | tf_op jit(solution)/shard_map/final/pallas_call | solution.py:252
  (8 shorter events, 0.1 us)
Async XLA Ops:
  0.6 61.7 %copy-start = (bf16[32,32]{1,0:T(8,128)(2,1)S(1)}, bf16[32,32]{1,0:T(8,128)(2,1)}, u32[]{:S(2)}) copy-start(bf16[32,32]{1,0:T(8,128)(2,1)} %param.12) | copy-start | bytes 6148
  0.6 60.7 %copy-start.3 = (f32[32]{0:T(128)S(1)}, f32[32]{0:T(128)}, u32[]{:S(2)}) copy-start(f32[32]{0:T(128)} %param.13) | copy-start | bytes 388
  18.4 30.3 %all-to-all-start = ((f32[16,1,16384]{2,1,0:T(1,128)}), f32[16,1,16384]{2,1,0:T(1,128)S(1)}, u32[]{:S(2)}, u32[]{:S(2)}) async-start(f32[16,1,16384]{2,1,0:T(1,128)} %bitcast.4), calls=%async_computation | async-start | bytes 2097152 | tf_op jit(solution)/shard_map/all_to_all | solution.py:298
  48.7 1.0 copy-start.2
  54.5 29.8 %all-to-all-start.1 = ((bf16[16,2,128,128]{3,2,1,0:T(8,128)(2,1)}), bf16[16,2,128,128]{3,2,1,0:T(8,128)(2,1)S(1)}, u32[]{:S(2)}, u32[]{:S(2)}) async-start(bf16[16,2,128,128]{3,2,1,0:T(8,128)(2,1)} %get-tuple-element.11), calls=%async_computation.1 | async-start | bytes 2097152 | tf_op jit(solution)/shard_map/all_to_all | solution.py:292
  159.2 29.8 %all-to-all-start.2 = ((f32[16,1,16384]{2,1,0:T(1,128)}), f32[16,1,16384]{2,1,0:T(1,128)S(1)}, u32[]{:S(2)}, u32[]{:S(2)}) async-start(f32[16,1,16384]{2,1,0:T(1,128)} %bitcast.10), calls=%async_computation.2 | async-start | bytes 2097152 | tf_op jit(solution)/shard_map/all_to_all | solution.py:310
  189.0 7.7 %copy-start.1 = (f32[16,1,16384]{2,1,0:T(1,128)}, f32[16,1,16384]{2,1,0:T(1,128)S(1)}, u32[]{:S(2)}) copy-start(f32[16,1,16384]{2,1,0:T(1,128)S(1)} %all-to-all-done.2) | copy-start | bytes 3145732
  189.8 14.8 %all-to-all-start.4 = ((f32[16,1,2048]{2,1,0:T(1,128)}), f32[16,1,2048]{2,1,0:T(1,128)S(1)}, u32[]{:S(2)}, u32[]{:S(2)}) async-start(f32[16,1,2048]{2,1,0:T(1,128)} %broadcast_in_dim.47), calls=%async_computation.4 | async-start | bytes 262144 | tf_op jit(solution)/shard_map/all_to_all | solution.py:311
  204.6 26.6 %all-to-all-start.3 = ((bf16[16,2,128,128]{3,2,1,0:T(8,128)(2,1)}), bf16[16,2,128,128]{3,2,1,0:T(8,128)(2,1)S(1)}, u32[]{:S(2)}, u32[]{:S(2)}) async-start(bf16[16,2,128,128]{3,2,1,0:T(8,128)(2,1)} %get-tuple-element.15), calls=%async_computation.3 | async-start | bytes 2097152 | tf_op jit(solution)/shard_map/all_to_all | solution.py:292
